TPU v7x, 512 devices: a whole 4x4x16 slice. The times are simulated.
512 devices in a mesh: lon: 64 (over x, y, z_hi, core), lat: 8 (over z_lo).
Axes of the slice: x: 4, y: 4, z: 16 (z_hi: 2, z_lo: 8; z = z_hi * 8 + z_lo), core: 2. Of those that a mesh axis runs over, the one named last changes fastest.
Arguments:
- sketch: float32 [64, 1024, 2048], P(None, 'lon', 'lat'), may hold values from -6 to 6
- probe_bits: int32 [2, 1024, 2048], P(None, 'lon', 'lat'), may hold values from 0 to 65535
- ocean: int32 [1024, 2048], P('lon', 'lat'), may hold values 0 or 1
- east_cond: float32 [1024, 2048], P('lon', 'lat'), may hold values from 0.2 to 2
- north_cond: float32 [1024, 2048], P('lon', 'lat'), may hold values from 0.1 to 1
- kappa_sq: float32 [1024, 2048], P('lon', 'lat'), may hold values from 0.05 to 0.5
- inv_area: float32 [1024, 2048], P('lon', 'lat'), may hold values from 0.05 to 0.2
Outputs:
- image_out: float32 [64, 1024, 2048], P(None, 'lon', 'lat')
- gram_out: float32 [96, 96], replicated
Inputs may be any that keep to these rules, and one draw needn't show every extreme that they name: `probe_bits`: each word holds 16 independent sign bits, bit b of word w giving probe column 16 w + b.
All inputs are finite; a program needn't handle non-finite values. No bound on the sum of `ocean` on one device may be relied on, other than what follows from the above.
Results may differ from a plain program's by a relative error of at most 0.00015.
Values sent between devices are 32-bit elements; how exact they have to be, the bound alone decides.
A program may use at most 64 MiB of HBM per device.

v0:
```python
import jax
import jax.numpy as jnp
from jax import lax
from jax.sharding import PartitionSpec as P


def padded_2(cells, sides, width, closed):
    for axis, dim in sides:
        count = lax.axis_size(axis)
        ends = count if closed else count - 1
        head = lax.slice_in_dim(cells, 0, width, axis=dim)
        tail = lax.slice_in_dim(cells, cells.shape[dim] - width, cells.shape[dim], axis=dim)
        cells = jnp.concatenate(
            [
                lax.ppermute(tail, axis, [(i, (i + 1) % count) for i in range(ends)]),
                cells,
                lax.ppermute(head, axis, [((i + 1) % count, i) for i in range(ends)]),
            ],
            axis=dim,
        )
    return cells


def sign_columns(probe_bits):
    shifts = jnp.arange(16, dtype=jnp.int32)
    picked = jnp.right_shift(probe_bits[:, None], shifts[None, :, None, None])
    flipped = jnp.bitwise_and(picked, 1)
    return (1 - 2 * flipped).astype(jnp.float32).reshape((-1,) + probe_bits.shape[1:])


def operate(padded, weights):
    middle = padded[:, 1:-1, 1:-1]
    return weights[0] * (
        weights[1] * middle
        - weights[2] * padded[:, 2:, 1:-1]
        - weights[3] * padded[:, :-2, 1:-1]
        - weights[4] * padded[:, 1:-1, 2:]
        - weights[5] * padded[:, 1:-1, :-2]
    )


def extend(field_in, thickness):
    wider = padded_2(field_in, (("lon", 1),), thickness, True)
    return padded_2(wider, (("lat", 2),), thickness, False)


def pair_gram(left, right):
    left_flat = left.reshape(left.shape[0], -1)
    right_flat = right.reshape(right.shape[0], -1)
    return jnp.einsum("ac,bc->ab", left_flat, right_flat, precision=lax.Precision.HIGHEST)


def local(sketch, probe_bits, ocean, east_cond, north_cond, kappa_sq, inv_area):
    lon_count, lat_count = ocean.shape
    sea_mask = ocean.astype(jnp.float32)
    stacked = jnp.stack([sea_mask, east_cond, north_cond, kappa_sq, inv_area])
    widened = padded_2(stacked, (("lon", 1),), 2, True)
    widened = padded_2(widened, (("lat", 2),), 2, False)
    sea_wide = widened[0]
    east_wide = widened[1]
    north_wide = widened[2]
    kappa_wide = widened[3]
    area_wide = widened[4]
    east_edges = east_wide[:-1] * sea_wide[:-1] * sea_wide[1:]
    north_edges = north_wide[:, :-1] * sea_wide[:, :-1] * sea_wide[:, 1:]

    def region(margin):
        offset = 2 - margin
        span_lon = lon_count + 2 * margin
        span_lat = lat_count + 2 * margin

        def window(array, shift_lon, shift_lat):
            return array[
                offset + shift_lon : offset + shift_lon + span_lon,
                offset + shift_lat : offset + shift_lat + span_lat,
            ]

        east_weight = window(east_edges, 0, 0)
        west_weight = window(east_edges, -1, 0)
        north_weight = window(north_edges, 0, 0)
        south_weight = window(north_edges, 0, -1)
        center_term = (
            window(kappa_wide, 0, 0) + east_weight + west_weight + north_weight + south_weight
        )
        return (
            window(sea_wide, 0, 0),
            center_term,
            east_weight,
            west_weight,
            north_weight,
            south_weight,
            window(area_wide, 0, 0),
        )

    interior = region(0)
    sketch_masked = sketch * sea_mask
    columns = jnp.concatenate([sketch_masked, sign_columns(probe_bits) * sea_mask], axis=0)
    sketch_count = sketch.shape[0]
    thickness = 2
    columns_wide = extend(columns, thickness)
    exterior = region(1)
    first_wide = operate(columns_wide, exterior)
    second = operate(first_wide * exterior[6], interior)
    local_gram = pair_gram(columns, second)
    summed = lax.psum(local_gram, ("lon", "lat"))
    cell_total = lax.axis_size("lon") * lon_count * lax.axis_size("lat") * lat_count
    return (second[:sketch_count], summed / cell_total)


def solution(mesh):
    in_specs = (
        P(None, "lon", "lat"),
        P(None, "lon", "lat"),
        P("lon", "lat"),
        P("lon", "lat"),
        P("lon", "lat"),
        P("lon", "lat"),
        P("lon", "lat"),
    )
    out_specs = (P(None, "lon", "lat"), P())
    return jax.shard_map(local, mesh=mesh, in_specs=in_specs, out_specs=out_specs, check_vma=False)
```

profile of v0, /device:TPU:1, one launch (start us, length us, event | category | flops | bytes accessed | tf_op | source)
XLA Modules:
  0.0 201.9 jit_solution(6590594522301561050)
XLA Ops:
  0.6 0.7 bitcast_dynamic-update-slice_fusion.4
  1.4 0.7 bitcast_dynamic-update-slice_fusion.3
  2.1 0.7 bitcast_dynamic-update-slice_fusion.2
  2.8 0.7 bitcast_dynamic-update-slice_fusion.1
  3.5 0.7 bitcast_dynamic-update-slice_fusion
  4.2 16.8 %collective-permute-start = (f32[5,2,256]{2,1,0:T(2,128)S(1)}, f32[5,2,256]{2,1,0:T(2,128)S(1)}, u32[]{:S(2)}, u32[]{:S(2)}) collective-permute-start(f32[5,2,256]{2,1,0:T(2,128)S(1)} %get-tuple-element.16), channel_id=1, source_target_pairs={{0,8},{8,16},{16,24},{24,32},{32,40},{40,48},{48,56},{56,64},{64,7... | collective-permute-start | bytes 30728 | tf_op jit(solution)/shard_map/ppermute | solution.py:15
  21.1 1.9 collective-permute-start.1
  23.0 0.7 convert_element_type.7
  23.7 1.8 copy_multiply_fusion
  25.6 0.1 shift_right_arithmetic.23
  25.7 0.8 copy.13
  26.4 0.2 fusion.24
  26.6 0.0 collective-permute-done
  26.6 8.1 %collective-permute-done.1 = f32[5,2,256]{2,1,0:T(2,128)S(1)} collective-permute-done((f32[5,2,256]{2,1,0:T(2,128)S(1)}, f32[5,2,256]{2,1,0:T(2,128)S(1)}, u32[]{:S(2)}, u32[]{:S(2)}) %collective-permute-start.1) | collective-permute-done | bytes 10272 | tf_op jit(solution)/shard_map/ppermute | solution.py:17
  34.8 0.1 fusion.34
  34.9 2.6 %collective-permute-start.2 = (f32[5,20,2]{2,1,0:T(8,128)S(1)}, f32[5,20,2]{2,1,0:T(8,128)S(1)}, u32[]{:S(2)}, u32[]{:S(2)}) collective-permute-start(f32[5,20,2]{2,1,0:T(8,128)S(1)} %get-tuple-element.14), channel_id=1, source_target_pairs={{0,1},{1,2},{2,3},{3,4},{4,5},{5,6},{6,7},{8,9},{9,10},{10,11},{11... | collective-permute-start | bytes 2408 | tf_op jit(solution)/shard_map/ppermute | solution.py:15
  37.5 1.3 collective-permute-start.3
  38.9 4.5 %collective-permute-start.4 = (f32[96,2,256]{2,0,1:T(8,128)S(1)}, f32[96,2,256]{2,0,1:T(8,128)S(1)}, u32[]{:S(2)}, u32[]{:S(2)}) collective-permute-start(f32[96,2,256]{2,0,1:T(8,128)S(1)} %get-tuple-element.8), channel_id=1, source_target_pairs={{0,8},{8,16},{16,24},{24,32},{32,40},{40,48},{48,56},{56,64},{64,7... | collective-permute-start | bytes 589832 | tf_op jit(solution)/shard_map/ppermute | solution.py:15
  43.4 1.9 collective-permute-start.5
  45.3 0.0 collective-permute-done.2
  45.3 0.0 collective-permute-done.3
  45.3 0.2 pad_maximum_fusion.12
  45.5 0.0 copy-start.5
  45.5 0.6 slice_bitcast_fusion.2
  46.2 0.1 slice_multiply_fusion.8
  46.3 0.8 fusion.27
  47.0 0.0 collective-permute-done.4
  47.0 0.0 copy-done.5
  47.0 0.0 copy-done.4
  47.0 0.0 copy-done.7
  47.1 0.0 copy-done.6
  47.1 0.0 copy-start
  47.1 15.5 %collective-permute-done.5 = f32[96,2,256]{2,0,1:T(8,128)S(1)} collective-permute-done((f32[96,2,256]{2,0,1:T(8,128)S(1)}, f32[96,2,256]{2,0,1:T(8,128)S(1)}, u32[]{:S(2)}, u32[]{:S(2)}) %collective-permute-start.5) | collective-permute-done | bytes 196640 | tf_op jit(solution)/shard_map/ppermute | solution.py:17
  62.6 0.1 pad_maximum_fusion.9
  62.7 0.3 fusion.33
  63.1 0.2 copy-done.2
  63.3 0.9 copy.15
  64.2 0.3 copy.14
  64.5 8.7 %collective-permute-start.6 = (f32[96,20,2]{0,2,1:T(2,128)S(1)}, f32[96,20,2]{0,2,1:T(2,128)}, u32[]{:S(2)}, u32[]{:S(2)}) collective-permute-start(f32[96,20,2]{0,2,1:T(2,128)S(1)} %copy.14), channel_id=1, source_target_pairs={{0,1},{1,2},{2,3},{3,4},{4,5},{5,6},{6,7},{8,9},{9,10},{10,11},{11... | collective-permute-start | bytes 46088 | tf_op jit(solution)/shard_map/ppermute | solution.py:15
  73.2 1.3 collective-permute-start.7
  74.5 1.5 fusion.31
  76.0 1.4 slice.182
  77.5 1.5 slice.196
  78.9 1.5 slice.208
  80.4 0.0 collective-permute-done.7
  80.4 0.4 copy.17
  80.8 0.0 collective-permute-done.6
  80.8 1.1 copy.16
  81.9 0.0 copy-start.3
  81.9 0.0 copy-start.8
  81.9 0.0 copy-start.9
  81.9 0.0 copy-start.10
  81.9 0.0 copy-start.11
  81.9 0.0 copy-start.12
  81.9 0.0 copy-start.13
  81.9 0.0 copy-start.14
  82.0 2.2 %pad_maximum_fusion = f32[96,20,260]{2,0,1:T(8,128)S(1)} fusion(f32[96,20,2]{2,0,1:T(8,128)S(1)} %copy.17, f32[96,2,256]{2,0,1:T(8,128)} %copy-done.2, f32[32,16,256]{2,0,1:T(8,128)S(1)} %fusion.24, f32[64,16,256]{2,0,1:T(8,128)S(1)} %copy_multiply_fusion, f32[96,2,256]{2,0,1:T(8,128)} %copy-done, f32[96,20,2]{2,0,1:T(8,128)S(1)} %copy.16), kind=kLoop, calls=%fused_computation | loop fusion | flops 2496000 | bytes 3993600 | tf_op jit(solution)/shard_map/concatenate | solution.py:13
  84.3 4.7 %fusion.3 = f32[96,18,258]{2,0,1:T(8,128)S(1)} fusion(f32[96,20,2]{2,0,1:T(8,128)S(1)} %copy.16, f32[96,2,256]{2,0,1:T(8,128)S(1)} %copy-done.3, f32[96,2,256]{2,0,1:T(8,128)S(1)} %copy-done.1, f32[32,16,256]{2,0,1:T(8,128)S(1)} %fusion.24, f32[64,16,256]{2,0,1:T(8,128)S(1)} %copy_multiply_fusion, f32[96,20,2]{2,0,1:T(8,128)S(1)} %copy.17, ...), kind=kLoop, calls=%fused_computation.5 | loop fusion | flops 8470656 | bytes 9260016 | tf_op jit(solution)/shard_map/mul | solution.py:103
  89.1 1.8 fusion.9
  90.9 1.4 fusion.17
  92.3 0.1 slice.214
  92.4 1.6 copy.20
  94.0 107.2 %psum.7 = f32[96,96]{1,0:T(8,128)S(1)} all-reduce(f32[96,96]{1,0:T(8,128)S(1)} %fusion.17), channel_id=1, replica_groups=mesh['lon'=64,'lat'=8] {'lon','lat'}, use_global_device_ids=true, to_apply=%region_0.0 | all-reduce | flops 9216 | bytes 73728 | tf_op jit(solution)/shard_map/psum | solution.py:105
  201.2 0.6 broadcast_multiply_fusion
  (30 shorter events, 0.1 us)
Async XLA Ops:
  4.2 22.4 %collective-permute-start = (f32[5,2,256]{2,1,0:T(2,128)S(1)}, f32[5,2,256]{2,1,0:T(2,128)S(1)}, u32[]{:S(2)}, u32[]{:S(2)}) collective-permute-start(f32[5,2,256]{2,1,0:T(2,128)S(1)} %get-tuple-element.16), channel_id=1, source_target_pairs={{0,8},{8,16},{16,24},{24,32},{32,40},{40,48},{48,56},{56,64},{64,7... | collective-permute-start | bytes 30728 | tf_op jit(solution)/shard_map/ppermute | solution.py:15
  21.1 13.7 %collective-permute-start.1 = (f32[5,2,256]{2,1,0:T(2,128)S(1)}, f32[5,2,256]{2,1,0:T(2,128)S(1)}, u32[]{:S(2)}, u32[]{:S(2)}) collective-permute-start(f32[5,2,256]{2,1,0:T(2,128)S(1)} %get-tuple-element.17), channel_id=1, source_target_pairs={{8,0},{16,8},{24,16},{32,24},{40,32},{48,40},{56,48},{64,56},{72,6... | collective-permute-start | bytes 30728 | tf_op jit(solution)/shard_map/ppermute | solution.py:17
  34.9 10.4 %collective-permute-start.2 = (f32[5,20,2]{2,1,0:T(8,128)S(1)}, f32[5,20,2]{2,1,0:T(8,128)S(1)}, u32[]{:S(2)}, u32[]{:S(2)}) collective-permute-start(f32[5,20,2]{2,1,0:T(8,128)S(1)} %get-tuple-element.14), channel_id=1, source_target_pairs={{0,1},{1,2},{2,3},{3,4},{4,5},{5,6},{6,7},{8,9},{9,10},{10,11},{11... | collective-permute-start | bytes 2408 | tf_op jit(solution)/shard_map/ppermute | solution.py:15
  37.5 7.8 %collective-permute-start.3 = (f32[5,20,2]{2,1,0:T(8,128)S(1)}, f32[5,20,2]{2,1,0:T(8,128)S(1)}, u32[]{:S(2)}, u32[]{:S(2)}) collective-permute-start(f32[5,20,2]{2,1,0:T(8,128)S(1)} %get-tuple-element.15), channel_id=1, source_target_pairs={{1,0},{2,1},{3,2},{4,3},{5,4},{6,5},{7,6},{9,8},{10,9},{11,10},{12... | collective-permute-start | bytes 2408 | tf_op jit(solution)/shard_map/ppermute | solution.py:17
  38.9 8.2 %collective-permute-start.4 = (f32[96,2,256]{2,0,1:T(8,128)S(1)}, f32[96,2,256]{2,0,1:T(8,128)S(1)}, u32[]{:S(2)}, u32[]{:S(2)}) collective-permute-start(f32[96,2,256]{2,0,1:T(8,128)S(1)} %get-tuple-element.8), channel_id=1, source_target_pairs={{0,8},{8,16},{16,24},{24,32},{32,40},{40,48},{48,56},{56,64},{64,7... | collective-permute-start | bytes 589832 | tf_op jit(solution)/shard_map/ppermute | solution.py:15
  43.4 19.2 %collective-permute-start.5 = (f32[96,2,256]{2,0,1:T(8,128)S(1)}, f32[96,2,256]{2,0,1:T(8,128)S(1)}, u32[]{:S(2)}, u32[]{:S(2)}) collective-permute-start(f32[96,2,256]{2,0,1:T(8,128)S(1)} %get-tuple-element.9), channel_id=1, source_target_pairs={{8,0},{16,8},{24,16},{32,24},{40,32},{48,40},{56,48},{64,56},{72,6... | collective-permute-start | bytes 589832 | tf_op jit(solution)/shard_map/ppermute | solution.py:17
  45.5 1.5 copy-start.5
  46.2 0.9 copy-start.4
  46.2 0.9 copy-start.7
  46.3 0.8 copy-start.6
  47.1 16.0 %copy-start = (f32[96,2,256]{2,0,1:T(8,128)}, f32[96,2,256]{2,0,1:T(8,128)S(1)}, u32[]{:S(2)}) copy-start(f32[96,2,256]{2,0,1:T(8,128)S(1)} %collective-permute-done.4) | copy-start | bytes 589828
  62.6 0.7 copy-start.2
  64.5 16.3 %collective-permute-start.6 = (f32[96,20,2]{0,2,1:T(2,128)S(1)}, f32[96,20,2]{0,2,1:T(2,128)}, u32[]{:S(2)}, u32[]{:S(2)}) collective-permute-start(f32[96,20,2]{0,2,1:T(2,128)S(1)} %copy.14), channel_id=1, source_target_pairs={{0,1},{1,2},{2,3},{3,4},{4,5},{5,6},{6,7},{8,9},{9,10},{10,11},{11... | collective-permute-start | bytes 46088 | tf_op jit(solution)/shard_map/ppermute | solution.py:15
  73.2 7.2 %collective-permute-start.7 = (f32[96,20,2]{0,2,1:T(2,128)}, f32[96,20,2]{0,2,1:T(2,128)S(1)}, u32[]{:S(2)}, u32[]{:S(2)}) collective-permute-start(f32[96,20,2]{0,2,1:T(2,128)} %copy.15), channel_id=1, source_target_pairs={{1,0},{2,1},{3,2},{4,3},{5,4},{6,5},{7,6},{9,8},{10,9},{11,10},{12... | collective-permute-start | bytes 46088 | tf_op jit(solution)/shard_map/ppermute | solution.py:17
  81.9 2.3 %copy-start.1 = (f32[96,2,256]{2,0,1:T(8,128)S(1)}, f32[96,2,256]{2,0,1:T(8,128)}, u32[]{:S(2)}) copy-start(f32[96,2,256]{2,0,1:T(8,128)} %copy-done) | copy-start | bytes 589828
  81.9 2.3 %copy-start.3 = (f32[96,2,256]{2,0,1:T(8,128)S(1)}, f32[96,2,256]{2,0,1:T(8,128)}, u32[]{:S(2)}) copy-start(f32[96,2,256]{2,0,1:T(8,128)} %copy-done.2) | copy-start | bytes 589828
  81.9 2.3 %copy-start.8 = (f32[18,258]{1,0:T(8,128)S(1)}, f32[18,258]{1,0:T(8,128)}, u32[]{:S(2)}) copy-start(f32[18,258]{1,0:T(8,128)} %get-tuple-element.23) | copy-start | bytes 55732
  81.9 2.3 %copy-start.9 = (f32[18,258]{1,0:T(8,128)S(1)}, f32[18,258]{1,0:T(8,128)}, u32[]{:S(2)}) copy-start(f32[18,258]{1,0:T(8,128)} %get-tuple-element.24) | copy-start | bytes 55732
  81.9 2.3 %copy-start.10 = (f32[18,258]{1,0:T(8,128)S(1)}, f32[18,258]{1,0:T(8,128)}, u32[]{:S(2)}) copy-start(f32[18,258]{1,0:T(8,128)} %get-tuple-element.25) | copy-start | bytes 55732
  81.9 2.3 %copy-start.11 = (f32[18,258]{1,0:T(8,128)S(1)}, f32[18,258]{1,0:T(8,128)}, u32[]{:S(2)}) copy-start(f32[18,258]{1,0:T(8,128)} %get-tuple-element.26) | copy-start | bytes 55732
  81.9 2.3 %copy-start.12 = (f32[18,258]{1,0:T(8,128)S(1)}, f32[18,258]{1,0:T(8,128)}, u32[]{:S(2)}) copy-start(f32[18,258]{1,0:T(8,128)} %get-tuple-element.27) | copy-start | bytes 55732
  81.9 2.3 %copy-start.13 = (f32[18,258]{1,0:T(8,128)S(1)}, f32[18,258]{1,0:T(8,128)}, u32[]{:S(2)}) copy-start(f32[18,258]{1,0:T(8,128)} %slice.196) | copy-start | bytes 55732
  81.9 2.3 %copy-start.14 = (f32[18,258]{1,0:T(8,128)S(1)}, f32[18,258]{1,0:T(8,128)}, u32[]{:S(2)}) copy-start(f32[18,258]{1,0:T(8,128)} %slice.208) | copy-start | bytes 55732
  84.3 4.8 %copy-start.15 = (f32[16,256]{1,0:T(8,128)S(1)}, f32[16,256]{1,0:T(8,128)}, u32[]{:S(2)}) copy-start(f32[16,256]{1,0:T(8,128)} %get-tuple-element.19) | copy-start | bytes 49156
  84.3 4.8 %copy-start.16 = (f32[16,256]{1,0:T(8,128)S(1)}, f32[16,256]{1,0:T(8,128)}, u32[]{:S(2)}) copy-start(f32[16,256]{1,0:T(8,128)} %get-tuple-element.20) | copy-start | bytes 49156
  84.3 4.8 %copy-start.17 = (f32[16,256]{1,0:T(8,128)S(1)}, f32[16,256]{1,0:T(8,128)}, u32[]{:S(2)}) copy-start(f32[16,256]{1,0:T(8,128)} %get-tuple-element.21) | copy-start | bytes 49156
  84.3 4.8 %copy-start.18 = (f32[16,256]{1,0:T(8,128)S(1)}, f32[16,256]{1,0:T(8,128)}, u32[]{:S(2)}) copy-start(f32[16,256]{1,0:T(8,128)} %get-tuple-element.22) | copy-start | bytes 49156
  84.3 4.8 %copy-start.19 = (f32[16,256]{1,0:T(8,128)S(1)}, f32[16,256]{1,0:T(8,128)}, u32[]{:S(2)}) copy-start(f32[16,256]{1,0:T(8,128)} %slice.182) | copy-start | bytes 49156
where the time goes:
time: 203 us; the launch traced here: 202 us
  blocking collectives  107 us (53%)
  starting transfers between devices  39.1 us (19%)
  waiting for transfers between devices  23.7 us (12%)
  other arithmetic  15.6 us (8%)
  local copies, waits for them, and re-layouts  13.8 us (7%)
    psum x1, blocking collectives, local(): summed = lax.psum(local_gram, ('lon', 'lat'))  107 us
    ppermute x4, starting transfers between devices, padded_2(): lax.ppermute(tail, axis, [(i, (i + 1) % count) for i in range(ends)])  32.7 us
    ppermute x4, waiting for transfers between devices, padded_2(): lax.ppermute(head, axis, [((i + 1) % count, i) for i in range(ends)])  23.7 us
    ppermute x4, starting transfers between devices, padded_2(): lax.ppermute(head, axis, [((i + 1) % count, i) for i in range(ends)])  6.41 us
    unnamed x45, local copies, waits for them, and re-layouts  4.79 us
    mul x1, other arithmetic, local(): second = operate(first_wide * exterior[6], interior)  4.75 us
    slice x3, local copies, waits for them, and re-layouts, window(): array[offset + shift_lon:offset + shift_lon + span_lon, offset + shift_la...  4.35 us
  transfers between devices with their start and end apart: 8, of which 2 were waited for; matrix products, arithmetic and copies ran while one was open for 6% of the time, Pallas kernels for 0%

commit v1 on v0

--- a/solution.py
+++ b/solution.py
@@ -102,7 +102,7 @@
     first_wide = operate(columns_wide, exterior)
     second = operate(first_wide * exterior[6], interior)
     local_gram = pair_gram(columns, second)
-    summed = lax.psum(local_gram, ("lon", "lat"))
+    summed = jnp.sum(lax.all_gather(local_gram, ("lon", "lat")), axis=0)
     cell_total = lax.axis_size("lon") * lon_count * lax.axis_size("lat") * lat_count
     return (second[:sketch_count], summed / cell_total)
 

time: 203 us -> 1570 us (7.73)
  waiting for transfers between devices: 23.7 us -> 1470 us
  blocking collectives: 107 us -> 0 us
    all_gather x0 -> x1, waiting for transfers between devices: none -> 1450 us  [local(): summed = jnp.sum(lax.all_gather(local_gram, ('lon', 'lat')), axis=0)]
    psum x1 -> x0, blocking collectives: 107 us -> none  [local(): summed = lax.psum(local_gram, ('lon', 'lat'))]
  transfers between devices with their start and end apart: 8 -> 9, of which waited for: 2 -> 3; matrix products, arithmetic and copies ran while one was open for 6% -> 1% of each run, Pallas kernels for 0% -> 0%
where the time goes in v1:
time: 1570 us
  waiting for transfers between devices  1470 us (94%)
  starting transfers between devices  39.1 us (2%)
  other arithmetic  25.7 us (2%)
    all_gather x1, waiting for transfers between devices, local(): summed = jnp.sum(lax.all_gather(local_gram, ('lon', 'lat')), axis=0)  1450 us
    ppermute x4, starting transfers between devices, padded_2(): lax.ppermute(tail, axis, [(i, (i + 1) % count) for i in range(ends)])  32.7 us
  transfers between devices with their start and end apart: 9, of which 3 were waited for; matrix products, arithmetic and copies ran while one was open for 1% of the time, Pallas kernels for 0%

profile of v1, /device:TPU:1, one launch (start us, length us, event | category | flops | bytes accessed | tf_op | source)
XLA Modules:
  0.0 1566.3 jit_solution(5231464782723708172)
XLA Ops:
  7.2 0.0 all-gather.3.cloned.1.call-start
  7.2 0.7 bitcast_dynamic-update-slice_fusion.4
  7.9 0.7 bitcast_dynamic-update-slice_fusion.3
  8.7 0.7 bitcast_dynamic-update-slice_fusion.2
  9.4 0.7 bitcast_dynamic-update-slice_fusion.1
  10.1 0.7 bitcast_dynamic-update-slice_fusion
  10.8 16.8 %collective-permute-start = (f32[5,2,256]{2,1,0:T(2,128)S(1)}, f32[5,2,256]{2,1,0:T(2,128)S(1)}, u32[]{:S(2)}, u32[]{:S(2)}) collective-permute-start(f32[5,2,256]{2,1,0:T(2,128)S(1)} %get-tuple-element.16), channel_id=1, source_target_pairs={{0,8},{8,16},{16,24},{24,32},{32,40},{40,48},{48,56},{56,64},{64,7... | collective-permute-start | bytes 30728 | tf_op jit(solution)/shard_map/ppermute | solution.py:15
  27.7 1.9 collective-permute-start.1
  29.6 0.7 convert_element_type.7
  30.3 1.8 copy_multiply_fusion
  32.2 0.1 shift_right_arithmetic.23
  32.2 0.8 copy.13
  33.0 0.2 fusion.24
  33.2 0.0 collective-permute-done
  33.2 8.1 collective-permute-done.1
  41.4 0.1 fusion.34
  41.5 2.6 collective-permute-start.2
  44.1 1.3 collective-permute-start.3
  45.5 4.5 collective-permute-start.4
  50.0 1.9 collective-permute-start.5
  51.9 0.0 collective-permute-done.2
  51.9 0.0 collective-permute-done.3
  51.9 0.2 pad_maximum_fusion.12
  52.1 0.0 copy-start.5
  52.1 0.6 slice_bitcast_fusion.2
  52.8 0.1 slice_multiply_fusion.8
  52.8 0.8 fusion.27
  53.6 0.0 collective-permute-done.4
  53.6 0.0 copy-done.5
  53.6 0.0 copy-done.7
  53.6 0.0 copy-done.6
  53.6 0.0 copy-start
  53.6 15.5 collective-permute-done.5
  69.2 0.1 pad_maximum_fusion.9
  69.3 0.3 fusion.33
  69.7 0.2 copy-done.2
  69.8 0.9 copy.15
  70.8 0.3 copy.14
  71.1 8.7 collective-permute-start.6
  79.8 1.3 collective-permute-start.7
  81.1 1.5 fusion.31
  82.6 1.4 slice.182
  84.1 1.5 slice.196
  85.5 1.5 slice.208
  87.0 0.0 collective-permute-done.7
  87.0 0.4 copy.17
  87.4 0.0 collective-permute-done.6
  87.4 1.1 copy.16
  88.5 0.0 copy-start.3
  88.5 2.2 pad_maximum_fusion
  90.8 0.0 copy-done.1
  90.8 0.0 copy-done.3
  90.8 0.0 copy-done.8
  90.8 0.0 copy-done.9
  90.8 0.0 copy-done.10
  90.9 4.7 fusion.3
  95.7 1.8 fusion.9
  97.5 2.0 fusion.17
  99.5 0.0 all-gather.3.cloned.1.call-update
  99.5 0.1 slice.214
  99.6 1.6 copy.20
  101.2 1447.5 %all-gather.3.cloned.1.call-done = f32[49152,96]{1,0:T(8,128)} async-done(((f32[96,96]{1,0:T(8,128)}), f32[49152,96]{1,0:T(8,128)}) %all-gather.3.cloned.1.call-update) | async-done | bytes 18874384 | tf_op jit(solution)/shard_map/all_gather | solution.py:105
  1548.7 10.1 reduce_sum.9
  1558.8 0.6 broadcast_multiply_fusion
  (33 shorter events, 0.1 us)
Async XLA Ops:
  7.2 1541.6 %all-gather.3.cloned.1.call-start = ((), (), s32[]{:S(2)}) async-start(), calls=%async_computation | async-start | bytes 25214976 | tf_op jit(solution)/shard_map/all_gather | solution.py:105
  10.8 22.4 %collective-permute-start = (f32[5,2,256]{2,1,0:T(2,128)S(1)}, f32[5,2,256]{2,1,0:T(2,128)S(1)}, u32[]{:S(2)}, u32[]{:S(2)}) collective-permute-start(f32[5,2,256]{2,1,0:T(2,128)S(1)} %get-tuple-element.16), channel_id=1, source_target_pairs={{0,8},{8,16},{16,24},{24,32},{32,40},{40,48},{48,56},{56,64},{64,7... | collective-permute-start | bytes 30728 | tf_op jit(solution)/shard_map/ppermute | solution.py:15
  27.7 13.7 collective-permute-start.1
  41.5 10.4 collective-permute-start.2
  44.1 7.8 collective-permute-start.3
  45.5 8.1 collective-permute-start.4
  50.0 19.2 %collective-permute-start.5 = (f32[96,2,256]{2,0,1:T(8,128)S(1)}, f32[96,2,256]{2,0,1:T(8,128)S(1)}, u32[]{:S(2)}, u32[]{:S(2)}) collective-permute-start(f32[96,2,256]{2,0,1:T(8,128)S(1)} %get-tuple-element.9), channel_id=1, source_target_pairs={{8,0},{16,8},{24,16},{32,24},{40,32},{48,40},{56,48},{64,56},{72,6... | collective-permute-start | bytes 589832 | tf_op jit(solution)/shard_map/ppermute | solution.py:17
  52.1 1.5 copy-start.5
  52.7 0.9 copy-start.4
  52.7 0.9 copy-start.7
  52.8 0.8 copy-start.6
  53.6 16.0 %copy-start = (f32[96,2,256]{2,0,1:T(8,128)}, f32[96,2,256]{2,0,1:T(8,128)S(1)}, u32[]{:S(2)}) copy-start(f32[96,2,256]{2,0,1:T(8,128)S(1)} %collective-permute-done.4) | copy-start | bytes 589828
  69.2 0.7 copy-start.2
  71.1 16.3 %collective-permute-start.6 = (f32[96,20,2]{0,2,1:T(2,128)S(1)}, f32[96,20,2]{0,2,1:T(2,128)}, u32[]{:S(2)}, u32[]{:S(2)}) collective-permute-start(f32[96,20,2]{0,2,1:T(2,128)S(1)} %copy.14), channel_id=1, source_target_pairs={{0,1},{1,2},{2,3},{3,4},{4,5},{5,6},{6,7},{8,9},{9,10},{10,11},{11... | collective-permute-start | bytes 46088 | tf_op jit(solution)/shard_map/ppermute | solution.py:15
  79.8 7.2 collective-permute-start.7
  88.5 2.3 copy-start.1
  88.5 2.3 copy-start.3
  88.5 2.3 copy-start.8
  88.5 2.3 copy-start.9
  88.5 2.3 copy-start.10
  88.5 2.3 copy-start.11
  88.5 2.3 copy-start.12
  88.5 2.3 copy-start.13
  88.5 2.3 copy-start.14
  90.9 4.8 copy-start.15
  90.9 4.8 copy-start.16
  90.9 4.8 copy-start.17
  90.9 4.8 copy-start.18
  90.9 4.8 copy-start.19
Sparse Core Ops, SparseCore 0:
  99.7 1449.0 all-gather.2
